TPU v7x, 256 devices: a whole 4x4x8 slice. The times are simulated.
256 devices in a mesh: tile: 32 (over z, y_hi, core), kern: 8 (over x, y_lo).
Axes of the slice: x: 4, y: 4 (y_hi: 2, y_lo: 2; y = y_hi * 2 + y_lo), z: 8, core: 2. Of those that a mesh axis runs over, the one named last changes fastest.
Arguments:
- mask_field: float32 [128, 32768], P(None, 'tile'), may hold values from 0 to 1
- target_image: int32 [128, 32768], P(None, 'tile'), may hold values 0 or 1
- kernels: float32 [24, 2, 61, 61], P('kern'), may hold values from -0.09375 to 0.09375
- kernel_weights: float32 [24], P('kern'), may hold values from 0.01 to 0.1
- live_list: int32 [32, 2], P('tile'), may hold values from 0 to 1, as said below
- live_count: int32 [32], P('tile'), may hold values from 1 to 2, as said below
Outputs:
- gradient: float32 [128, 32768], P('kern', 'tile')
Inputs may be any that keep to these rules, and one draw needn't show every extreme that they name: `live_count`: every strip has at least one non-empty tile and some strip has all 2 slots non-empty. `live_list`: each row is a permutation of the slots 0 to 1; its first live_count entries are the strip's non-empty slots in increasing order.
All inputs are finite; a program needn't handle non-finite values. No bound on the sum of `target_image` on one device may be relied on, other than what follows from the above.
Results may differ from a plain program's by a relative error of at most 0.00015.
Values sent between devices are 32-bit elements; how exact they have to be, the bound alone decides.
A program may use at most 128 MiB of HBM per device.

v0:
```python
import functools

import jax
import jax.numpy as jnp
import ml_dtypes
import numpy as np
from jax import lax
from jax.experimental import pallas as pl
from jax.experimental.pallas import tpu as pltpu
from jax.sharding import PartitionSpec as P

MESH = pl.DeviceIdType.MESH
steepness = 4.0
threshold = 0.6

ROWS = 128
BLOCK = 128
RIM = 30
SUP = 61
PERIOD_R = 159
FREQ_R = 80
PERIOD_C = 255
FREQ_C = 128
SIDE = 64


def split_np(table):
    hi = table.astype(np.float32).astype(ml_dtypes.bfloat16)
    lo = (table - hi.astype(np.float64)).astype(np.float32).astype(ml_dtypes.bfloat16)
    return hi, lo


def phases(first, second, period):
    angle = 2.0 * np.pi / period * (np.outer(first, second) % period)
    return np.cos(angle), np.sin(angle)


@functools.cache
def tables():
    fr, fc = np.arange(FREQ_R), np.arange(FREQ_C)
    rows, window = np.arange(ROWS), np.arange(2 * BLOCK)
    taps = np.arange(SUP) - RIM
    row_weight = np.where(fr == 0, 1.0, 2.0) / PERIOD_R
    col_weight = np.where(fc == 0, 1.0, 2.0) / PERIOD_C * 0.5
    c, s = phases(fr, rows, PERIOD_R)
    to_rows_hi, to_rows_lo = split_np(np.concatenate([c, s], 0))
    row_forward = np.concatenate([to_rows_hi, to_rows_hi, to_rows_lo], 1)
    back = np.concatenate([c * row_weight[:, None], s * row_weight[:, None]], 0).T
    back_hi, back_lo = split_np(back)
    row_back = np.concatenate([back_hi, back_hi, back_lo], 1)
    c, s = phases(window, fc, PERIOD_C)
    col_hi, col_lo = split_np(np.concatenate([c, s], 1))
    inv = np.concatenate([(c * col_weight).T, (s * col_weight).T], 0)
    inv_hi, inv_lo = split_np(inv)
    mid = slice(SIDE, SIDE + BLOCK)
    inv_mid = np.concatenate([inv_hi[:, mid], inv_lo[:, mid]], 1)
    src_hi = np.concatenate([col_hi[mid], col_hi[mid], col_lo[mid]], 0)
    c, s = phases(taps, fc, PERIOD_C)
    tap_cols = np.zeros((64, 2 * FREQ_C))
    tap_cols[:SUP] = np.concatenate([c, s], 1)
    tc_hi, tc_lo = split_np(tap_cols)
    zero = np.zeros_like(tc_hi)

    def pair(t):
        return np.concatenate(
            [np.concatenate([t, zero], 1), np.concatenate([zero, t], 1)], 0
        )

    tap_col = np.concatenate([pair(tc_hi), pair(tc_hi), pair(tc_lo)], 0)
    c, s = phases(fr, taps, PERIOD_R)
    tap_rows = np.zeros((2 * FREQ_R, 64))
    tap_rows[:, :SUP] = np.concatenate([c, s], 0)
    tr_hi, tr_lo = split_np(tap_rows)
    tap_row = np.concatenate([tr_hi, tr_hi, tr_lo], 1)
    return (row_forward, row_back, col_hi, col_lo, inv_hi, inv_lo, inv_mid, src_hi, tap_col, tap_row)


def split(value):
    hi = value.astype(jnp.bfloat16)
    lo = (value - hi.astype(jnp.float32)).astype(jnp.bfloat16)
    return hi, lo


def dot(a, b):
    return jnp.dot(a, b, preferred_element_type=jnp.float32)


def dot3(a, b_hi, b_lo):
    a_hi, a_lo = split(a)
    return dot(a_hi, b_hi) + (dot(a_lo, b_hi) + dot(a_hi, b_lo))


def stacked(value):
    hi, lo = split(value)
    return jnp.concatenate([hi, lo, hi], 0)


def quarters(spec):
    cc, cs = spec[:FREQ_R, :FREQ_C], spec[:FREQ_R, FREQ_C:]
    sc, ss = spec[FREQ_R:, :FREQ_C], spec[FREQ_R:, FREQ_C:]
    return cc - ss, cs + sc, cc + ss, sc - cs


def unquarters(ur, ui, vr, vi):
    top = jnp.concatenate([ur + vr, ui - vi], 1)
    bottom = jnp.concatenate([ui + vi, vr - ur], 1)
    return jnp.concatenate([top, bottom], 0)


def body(
    strips, parts, local,
    mask_ref, target_ref, kern_ref, weight_ref, list_ref, count_ref,
    row_forward, row_back, col_hi, col_lo, inv_hi, inv_lo, inv_mid, src_tab, tap_col, tap_row,
    out_ref,
    kbuf, halo_src, halo_left, halo_right, xspec, spec, fields, inten, gspec, gwin, rbuf, edge_left, edge_right, acc,
    k_send, k_recv, h_send, h_recv, g_send, g_recv, e_send, e_recv,
):
    t = lax.axis_index("tile")
    j = lax.axis_index("kern")
    up = lax.rem(t + 1, strips)
    down = lax.rem(t + strips - 1, strips)
    chunk = ROWS // parts
    first, last = j == 0, j == parts - 1

    barrier = pltpu.get_barrier_semaphore()
    for d in range(1, parts):
        pl.semaphore_signal(barrier, inc=1, device_id=(t, lax.rem(j + d, parts)), device_id_type=MESH)
    pl.semaphore_signal(barrier, inc=1, device_id=(up, 0), device_id_type=MESH)
    pl.semaphore_signal(barrier, inc=1, device_id=(down, parts - 1), device_id_type=MESH)

    kbuf[0] = jnp.zeros_like(kbuf[0])
    for k in range(local):
        kbuf[0, 64 * k : 64 * k + SUP, 0:SUP] = kern_ref[k, 0]
        kbuf[0, 64 * k : 64 * k + SUP, 64 : 64 + SUP] = kern_ref[k, 1]
        kbuf[0, 64 * k + SUP : 64 * k + SUP + 1, :] = jnp.full((1, 128), weight_ref[k], jnp.float32)

    def flag(slot):
        found = jnp.float32(0.0)
        for place in range(2):
            hit = (list_ref[0, place] == slot) & (place < count_ref[0])
            found = jnp.where(hit, jnp.float32(1.0), found)
        return found

    half = ROWS // 2
    live_rows = jnp.concatenate(
        [jnp.full((half, 128), flag(0), jnp.float32), jnp.full((half, 128), flag(1), jnp.float32)], 0
    )

    def column(index):
        return mask_ref[:, pl.ds(pl.multiple_of(index * 128, 128), 128)] * live_rows

    halo_src[...] = jnp.where(first, column(0), column(parts - 1))

    @pl.when(first)
    def _():
        pl.semaphore_wait(barrier, 2 * parts - 1)

    @pl.when(last)
    def _():
        pl.semaphore_wait(barrier, 2 * parts - 1)

    @pl.when(jnp.logical_not(first | last))
    def _():
        pl.semaphore_wait(barrier, parts - 1)

    def to_down():
        return pltpu.make_async_remote_copy(
            halo_src, halo_right, h_send.at[0], h_recv.at[0],
            device_id=(down, parts - 1), device_id_type=MESH)

    def to_up():
        return pltpu.make_async_remote_copy(
            halo_src, halo_left, h_send.at[0], h_recv.at[0],
            device_id=(up, 0), device_id_type=MESH)

    @pl.when(first)
    def _():
        to_down().start()

    @pl.when(last)
    def _():
        to_up().start()

    def kern_copy(d):
        return pltpu.make_async_remote_copy(
            kbuf.at[0], kbuf.at[d], k_send.at[d], k_recv.at[d],
            device_id=(t, lax.rem(j + d, parts)), device_id_type=MESH)

    for d in range(1, parts):
        kern_copy(d).start()

    @pl.when(first)
    def _():
        to_down().wait()

    @pl.when(last)
    def _():
        to_up().wait()

    before = jnp.where(
        first,
        jnp.where(t > 0, halo_left[...], 0.0),
        column(jnp.maximum(j - 1, 0)),
    )
    after = jnp.where(
        last,
        jnp.where(t < strips - 1, halo_right[...], 0.0),
        column(jnp.minimum(j + 1, parts - 1)),
    )
    here = column(j)
    window = jnp.concatenate([before[:, SIDE:], here, after[:, :SIDE]], 1)
    by_rows = dot(row_forward[...], stacked(window))
    spectrum = dot3(by_rows, col_hi[...], col_lo[...])
    for place, piece in enumerate(quarters(spectrum)):
        xspec[place] = piece

    inten[...] = jnp.zeros_like(inten)

    def forward(d, carry):
        @pl.when(d > 0)
        def _():
            kern_copy(d).wait()

        k_hi, k_lo = split(kbuf[d])
        taps = dot(jnp.concatenate([k_hi, k_lo], 1), tap_col[0:256, :]) + dot(k_hi, tap_col[256:384, :])
        t_hi, t_lo = split(taps)
        for k in range(local):
            place = d * local + k
            rows = slice(64 * k, 64 * k + 64)
            both = dot(tap_row[...], jnp.concatenate([t_hi[rows], t_lo[rows], t_hi[rows]], 0))
            products = []
            for part in range(2):
                lanes = slice(part * 128, part * 128 + 128)
                ur, ui, vr, vi = quarters(both[:, part * 256 : part * 256 + 256])
                spec[place, 0, :, lanes] = ur
                spec[place, 1, :, lanes] = ui
                spec[place, 2, :, lanes] = vr
                spec[place, 3, :, lanes] = vi
                xur, xui, xvr, xvi = xspec[0], xspec[1], xspec[2], xspec[3]
                products.append(
                    unquarters(
                        ur * xur - ui * xui, ur * xui + ui * xur,
                        vr * xvr - vi * xvi, vr * xvi + vi * xvr,
                    )
                )
            y_hi, y_lo = split(jnp.concatenate(products, 0))
            wide = dot(y_hi, inv_mid[...])
            inner = wide[:, :128] + (wide[:, 128:] + dot(y_lo, inv_mid[:, :128]))
            n = 2 * FREQ_R
            field = dot(row_back[...], stacked(jnp.concatenate([inner[:n], inner[n:]], 1)))
            fields[place] = field
            weight = kbuf[d, 64 * k + SUP : 64 * k + SUP + 1, :]
            real, imag = field[:, :128], field[:, 128:]
            inten[...] += weight * (real * real + imag * imag)
        return carry

    lax.fori_loop(0, parts, forward, 0)

    printed = jax.nn.sigmoid(steepness * (inten[...] - threshold))
    target = target_ref[:, pl.ds(pl.multiple_of(j * 128, 128), 128)].astype(jnp.float32)
    inten[...] = live_rows * (4.0 * steepness) * (printed - target) * printed * (1.0 - printed)
    gspec[...] = jnp.zeros_like(gspec)

    def adjoint(d, carry):
        for k in range(local):
            place = d * local + k
            weight = kbuf[d, 64 * k + SUP : 64 * k + SUP + 1, :]
            slope = inten[...] * weight
            source = fields[place] * jnp.concatenate([slope, slope], 1)
            by_rows = dot(row_forward[...], stacked(source))
            pair = jnp.concatenate([by_rows[:, :128], by_rows[:, 128:]], 0)
            s_hi, s_lo = split(pair)
            found = dot(jnp.concatenate([s_hi, s_lo], 1), src_tab[0:256, :]) + dot(s_hi, src_tab[256:384, :])
            n = 2 * FREQ_R
            for part in range(2):
                lanes = slice(part * 128, part * 128 + 128)
                sur, sui, svr, svi = quarters(found[part * n : part * n + n])
                ur, ui = spec[place, 0, :, lanes], spec[place, 1, :, lanes]
                vr, vi = spec[place, 2, :, lanes], spec[place, 3, :, lanes]
                gspec[0] += sur * ur + sui * ui
                gspec[1] += sui * ur - sur * ui
                gspec[2] += svr * vr + svi * vi
                gspec[3] += svi * vr - svr * vi
        return carry

    lax.fori_loop(0, parts, adjoint, 0)

    total = unquarters(gspec[0], gspec[1], gspec[2], gspec[3])
    inner = dot3(total, inv_hi[...], inv_lo[...])
    gwin[...] = dot(row_back[...], stacked(inner))

    def rows_of(index):
        return pl.ds(pl.multiple_of(index * chunk, chunk), chunk)

    def grad_copy(d):
        other = lax.rem(j + d, parts)
        return pltpu.make_async_remote_copy(
            gwin.at[rows_of(other), :], rbuf.at[d], g_send.at[d], g_recv.at[d],
            device_id=(t, other), device_id_type=MESH)

    def edge_down(i):
        return pltpu.make_async_remote_copy(
            gwin.at[i * chunk : (i + 1) * chunk, 0:128], edge_right, e_send.at[i], e_recv.at[0],
            device_id=(down, i), device_id_type=MESH)

    def edge_up(i):
        return pltpu.make_async_remote_copy(
            gwin.at[i * chunk : (i + 1) * chunk, 128:256], edge_left, e_send.at[i], e_recv.at[1],
            device_id=(up, i), device_id_type=MESH)

    @pl.when(first)
    def _():
        for i in range(parts):
            edge_down(i).start()

    @pl.when(last)
    def _():
        for i in range(parts):
            edge_up(i).start()

    for d in range(1, parts):
        grad_copy(d).start()

    acc[...] = jnp.zeros_like(acc)
    acc[:, pl.ds(pl.multiple_of(j * 128, 128), 256)] += gwin[rows_of(j), :]
    for d in range(1, parts):
        grad_copy(d).wait_recv()
        source = lax.rem(j + parts - d, parts)
        acc[:, pl.ds(pl.multiple_of(source * 128, 128), 256)] += rbuf[d]
    edge_down(0).wait_recv()
    edge_up(0).wait_recv()
    acc[:, BLOCK * parts :] += jnp.where(t < strips - 1, edge_right[...], 0.0)
    acc[:, 0:128] += jnp.where(t > 0, edge_left[...], 0.0)
    half_parts = parts // 2
    mine = jnp.where(j < half_parts, flag(0), flag(1))
    out_ref[...] = acc[:, SIDE : SIDE + BLOCK * parts] * mine

    for d in range(1, parts):
        grad_copy(d).wait_send()

    @pl.when(first)
    def _():
        for i in range(parts):
            edge_down(i).wait_send()

    @pl.when(last)
    def _():
        for i in range(parts):
            edge_up(i).wait_send()


def shards(mask_field, target_image, kernels, kernel_weights, live_list, live_count):
    strips, parts = lax.axis_size("tile"), lax.axis_size("kern")
    local = kernels.shape[0]
    count = local * parts
    vmem = pl.BlockSpec(memory_space=pltpu.VMEM)
    smem = pl.BlockSpec(memory_space=pltpu.SMEM)
    f32 = jnp.float32
    chunk = ROWS // parts
    consts = tables()
    return pl.pallas_call(
        functools.partial(body, strips, parts, local),
        out_shape=jax.ShapeDtypeStruct((chunk, BLOCK * parts), f32),
        in_specs=[vmem, vmem, vmem, smem, smem, smem] + [vmem] * len(consts),
        out_specs=vmem,
        scratch_shapes=[
            pltpu.VMEM((parts, 64 * local, 128), f32),
            pltpu.VMEM((ROWS, 128), f32),
            pltpu.VMEM((ROWS, 128), f32),
            pltpu.VMEM((ROWS, 128), f32),
            pltpu.VMEM((4, FREQ_R, FREQ_C), f32),
            pltpu.VMEM((count, 4, FREQ_R, 2 * FREQ_C), f32),
            pltpu.VMEM((count, ROWS, 256), f32),
            pltpu.VMEM((ROWS, 128), f32),
            pltpu.VMEM((4, FREQ_R, FREQ_C), f32),
            pltpu.VMEM((ROWS, 256), f32),
            pltpu.VMEM((parts, chunk, 256), f32),
            pltpu.VMEM((chunk, 128), f32),
            pltpu.VMEM((chunk, 128), f32),
            pltpu.VMEM((chunk, BLOCK * parts + 128), f32),
            pltpu.SemaphoreType.DMA((parts,)),
            pltpu.SemaphoreType.DMA((parts,)),
            pltpu.SemaphoreType.DMA((1,)),
            pltpu.SemaphoreType.DMA((1,)),
            pltpu.SemaphoreType.DMA((parts,)),
            pltpu.SemaphoreType.DMA((parts,)),
            pltpu.SemaphoreType.DMA((parts,)),
            pltpu.SemaphoreType.DMA((2,)),
        ],
        compiler_params=pltpu.CompilerParams(
            collective_id=0, has_side_effects=True, vmem_limit_bytes=56 * 1024 * 1024
        ),
    )(mask_field, target_image, kernels, kernel_weights, live_list, live_count, *consts)


def solution(mesh):
    placed = (
        P(None, "tile"),
        P(None, "tile"),
        P("kern", None, None, None),
        P("kern"),
        P("tile", None),
        P("tile"),
    )
    return jax.shard_map(
        shards, mesh=mesh, in_specs=placed, out_specs=P("kern", "tile"), check_vma=False
    )
```

profile of v0, /device:TPU:2, one launch (start us, length us, event | category | flops | bytes accessed | tf_op | source)
XLA Modules:
  0.0 45.6 jit_solution(3520353681284237376)
XLA Ops:
  0.7 1.6 %copy.17.kern_ref = f32[3,2,61,61]{3,2,1,0:T(8,128)} copy(f32[3,2,61,61]{3,1,2,0:T(2,128)} %param.18) | data formatting | bytes 178608 | tf_op args[2]
  2.3 41.9 %shard_map.154 = f32[16,1024]{1,0:T(8,128)} custom-call(f32[128,1024]{1,0:T(8,128)} %mask_ref.1, s32[128,1024]{1,0:T(8,128)} %target_ref.1, f32[3,2,61,61]{3,2,1,0:T(8,128)} %copy.17.kern_ref, f32[3]{0:T(128)} %weight_ref.1, s32[1,2]{1,0:T(1,128)} %list_ref.1, s32[1]{0:T(128)S(6)} %copy.19.count_ref, bf16[160,384]{1,0:T(8,128)(2,1)} %constant.20.clone.row_forward, ...), custom_call_target="tpu_custom_call" | custom-call | tf_op jit(solution)/shard_map/pallas_call | solution.py:361
  44.2 1.5 %copy.20 = f32[16,1024]{1,0:T(8,128)} copy(f32[16,1024]{1,0:T(8,128)} %shard_map.154) | data formatting | bytes 131072
where the time goes:
time: 45.8 us; the launch traced here: 45.6 us
  Pallas kernels  41.9 us (91%)
  local copies, waits for them, and re-layouts  3.09 us (7%)
  between operations  0.66 us (1%)
    pallas_call x1, Pallas kernels, shards(): pl.pallas_call(functools.partial(body, strips, parts, local), out_shape=j...  41.9 us
    unnamed x2, local copies, waits for them, and re-layouts  3.09 us

commit v1 on v0

--- a/solution.py
+++ b/solution.py
@@ -109,9 +109,19 @@
 
 def body(
     strips, parts, local,
-    mask_ref, target_ref, kern_ref, weight_ref, list_ref, count_ref,
-    row_forward, row_back, col_hi, col_lo, inv_hi, inv_lo, inv_mid, src_tab, tap_col, tap_row,
-    out_ref,
+    mask_ref, target_ref, kern_ref, weight_ref, list_ref, count_ref, *rest,
+):
+    table_count = len(tables())
+    in_hbm, rest = rest[:table_count], rest[table_count:]
+    out_ref, rest = rest[0], rest[1:]
+    held, rest = rest[:table_count], rest[table_count:]
+    run(strips, parts, local, mask_ref, target_ref, kern_ref, weight_ref, list_ref, count_ref, in_hbm, out_ref, held, *rest)
+
+
+def run(
+    strips, parts, local,
+    mask_ref, target_ref, kern_ref, weight_ref, list_ref, count_ref, in_hbm, out_ref, held,
+    raw, mwin, twin, l_sem, t_sem,
     kbuf, halo_src, halo_left, halo_right, xspec, spec, fields, inten, gspec, gwin, rbuf, edge_left, edge_right, acc,
     k_send, k_recv, h_send, h_recv, g_send, g_recv, e_send, e_recv,
 ):
@@ -121,17 +131,46 @@
     down = lax.rem(t + strips - 1, strips)
     chunk = ROWS // parts
     first, last = j == 0, j == parts - 1
+    has_up, has_down = t < strips - 1, t > 0
+    sends_up, sends_down = last & has_up, first & has_down
+    row_forward, row_back, col_hi, col_lo, inv_hi, inv_lo, inv_mid, src_tab, tap_col, tap_row = held
+
+    def strip_column(ref, index):
+        return ref.at[:, pl.ds(pl.multiple_of(index * 128, 128), 128)]
+
+    kern_load = pltpu.make_async_copy(kern_ref, raw, l_sem.at[0])
+    kern_load.start()
+    loads = [
+        pltpu.make_async_copy(strip_column(mask_ref, j), mwin.at[1], l_sem.at[2]),
+        pltpu.make_async_copy(strip_column(mask_ref, jnp.maximum(j - 1, 0)), mwin.at[0], l_sem.at[1]),
+        pltpu.make_async_copy(strip_column(mask_ref, jnp.minimum(j + 1, parts - 1)), mwin.at[2], l_sem.at[3]),
+        pltpu.make_async_copy(strip_column(target_ref, j), twin, l_sem.at[4]),
+    ]
+    for load in loads:
+        load.start()
+    table_loads = [
+        pltpu.make_async_copy(source, place, t_sem.at[i]) for i, (source, place) in enumerate(zip(in_hbm, held))
+    ]
+    for load in table_loads:
+        load.start()
 
     barrier = pltpu.get_barrier_semaphore()
     for d in range(1, parts):
         pl.semaphore_signal(barrier, inc=1, device_id=(t, lax.rem(j + d, parts)), device_id_type=MESH)
-    pl.semaphore_signal(barrier, inc=1, device_id=(up, 0), device_id_type=MESH)
-    pl.semaphore_signal(barrier, inc=1, device_id=(down, parts - 1), device_id_type=MESH)
+
+    @pl.when(has_up)
+    def _():
+        pl.semaphore_signal(barrier, inc=1, device_id=(up, 0), device_id_type=MESH)
+
+    @pl.when(has_down)
+    def _():
+        pl.semaphore_signal(barrier, inc=1, device_id=(down, parts - 1), device_id_type=MESH)
 
     kbuf[0] = jnp.zeros_like(kbuf[0])
+    kern_load.wait()
     for k in range(local):
-        kbuf[0, 64 * k : 64 * k + SUP, 0:SUP] = kern_ref[k, 0]
-        kbuf[0, 64 * k : 64 * k + SUP, 64 : 64 + SUP] = kern_ref[k, 1]
+        kbuf[0, 64 * k : 64 * k + SUP, 0:SUP] = raw[k, 0]
+        kbuf[0, 64 * k : 64 * k + SUP, 64 : 64 + SUP] = raw[k, 1]
         kbuf[0, 64 * k + SUP : 64 * k + SUP + 1, :] = jnp.full((1, 128), weight_ref[k], jnp.float32)
 
     def flag(slot):
@@ -146,20 +185,18 @@
         [jnp.full((half, 128), flag(0), jnp.float32), jnp.full((half, 128), flag(1), jnp.float32)], 0
     )
 
-    def column(index):
-        return mask_ref[:, pl.ds(pl.multiple_of(index * 128, 128), 128)] * live_rows
-
-    halo_src[...] = jnp.where(first, column(0), column(parts - 1))
-
-    @pl.when(first)
+    for load in loads[:3]:
+        load.wait()
+    here = mwin[1] * live_rows
+    halo_src[...] = here
+
+    edge_device = sends_up | sends_down
+
+    @pl.when(edge_device)
     def _():
         pl.semaphore_wait(barrier, 2 * parts - 1)
 
-    @pl.when(last)
-    def _():
-        pl.semaphore_wait(barrier, 2 * parts - 1)
-
-    @pl.when(jnp.logical_not(first | last))
+    @pl.when(jnp.logical_not(edge_device))
     def _():
         pl.semaphore_wait(barrier, parts - 1)
 
@@ -173,11 +210,11 @@
             halo_src, halo_left, h_send.at[0], h_recv.at[0],
             device_id=(up, 0), device_id_type=MESH)
 
-    @pl.when(first)
+    @pl.when(sends_down)
     def _():
         to_down().start()
 
-    @pl.when(last)
+    @pl.when(sends_up)
     def _():
         to_up().start()
 
@@ -189,25 +226,18 @@
     for d in range(1, parts):
         kern_copy(d).start()
 
-    @pl.when(first)
+    @pl.when(sends_down)
     def _():
         to_down().wait()
 
-    @pl.when(last)
+    @pl.when(sends_up)
     def _():
         to_up().wait()
 
-    before = jnp.where(
-        first,
-        jnp.where(t > 0, halo_left[...], 0.0),
-        column(jnp.maximum(j - 1, 0)),
-    )
-    after = jnp.where(
-        last,
-        jnp.where(t < strips - 1, halo_right[...], 0.0),
-        column(jnp.minimum(j + 1, parts - 1)),
-    )
-    here = column(j)
+    before = jnp.where(first, jnp.where(has_down, halo_left[...], 0.0), mwin[0] * live_rows)
+    after = jnp.where(last, jnp.where(has_up, halo_right[...], 0.0), mwin[2] * live_rows)
+    for load in table_loads:
+        load.wait()
     window = jnp.concatenate([before[:, SIDE:], here, after[:, :SIDE]], 1)
     by_rows = dot(row_forward[...], stacked(window))
     spectrum = dot3(by_rows, col_hi[...], col_lo[...])
@@ -257,7 +287,8 @@
     lax.fori_loop(0, parts, forward, 0)
 
     printed = jax.nn.sigmoid(steepness * (inten[...] - threshold))
-    target = target_ref[:, pl.ds(pl.multiple_of(j * 128, 128), 128)].astype(jnp.float32)
+    loads[3].wait()
+    target = twin[...].astype(jnp.float32)
     inten[...] = live_rows * (4.0 * steepness) * (printed - target) * printed * (1.0 - printed)
     gspec[...] = jnp.zeros_like(gspec)
 
@@ -308,12 +339,12 @@
             gwin.at[i * chunk : (i + 1) * chunk, 128:256], edge_left, e_send.at[i], e_recv.at[1],
             device_id=(up, i), device_id_type=MESH)
 
-    @pl.when(first)
+    @pl.when(sends_down)
     def _():
         for i in range(parts):
             edge_down(i).start()
 
-    @pl.when(last)
+    @pl.when(sends_up)
     def _():
         for i in range(parts):
             edge_up(i).start()
@@ -327,10 +358,17 @@
         grad_copy(d).wait_recv()
         source = lax.rem(j + parts - d, parts)
         acc[:, pl.ds(pl.multiple_of(source * 128, 128), 256)] += rbuf[d]
-    edge_down(0).wait_recv()
-    edge_up(0).wait_recv()
-    acc[:, BLOCK * parts :] += jnp.where(t < strips - 1, edge_right[...], 0.0)
-    acc[:, 0:128] += jnp.where(t > 0, edge_left[...], 0.0)
+
+    @pl.when(has_up)
+    def _():
+        edge_down(0).wait_recv()
+        acc[:, BLOCK * parts :] += edge_right[...]
+
+    @pl.when(has_down)
+    def _():
+        edge_up(0).wait_recv()
+        acc[:, 0:128] += edge_left[...]
+
     half_parts = parts // 2
     mine = jnp.where(j < half_parts, flag(0), flag(1))
     out_ref[...] = acc[:, SIDE : SIDE + BLOCK * parts] * mine
@@ -338,12 +376,12 @@
     for d in range(1, parts):
         grad_copy(d).wait_send()
 
-    @pl.when(first)
+    @pl.when(sends_down)
     def _():
         for i in range(parts):
             edge_down(i).wait_send()
 
-    @pl.when(last)
+    @pl.when(sends_up)
     def _():
         for i in range(parts):
             edge_up(i).wait_send()
@@ -355,15 +393,22 @@
     count = local * parts
     vmem = pl.BlockSpec(memory_space=pltpu.VMEM)
     smem = pl.BlockSpec(memory_space=pltpu.SMEM)
+    hbm = pl.BlockSpec(memory_space=pl.ANY)
     f32 = jnp.float32
     chunk = ROWS // parts
     consts = tables()
     return pl.pallas_call(
         functools.partial(body, strips, parts, local),
         out_shape=jax.ShapeDtypeStruct((chunk, BLOCK * parts), f32),
-        in_specs=[vmem, vmem, vmem, smem, smem, smem] + [vmem] * len(consts),
+        in_specs=[hbm, hbm, hbm, smem, smem, smem] + [hbm] * len(consts),
         out_specs=vmem,
-        scratch_shapes=[
+        scratch_shapes=[pltpu.VMEM(c.shape, jnp.bfloat16) for c in consts]
+        + [
+            pltpu.VMEM(kernels.shape, f32),
+            pltpu.VMEM((3, ROWS, 128), f32),
+            pltpu.VMEM((ROWS, 128), jnp.int32),
+            pltpu.SemaphoreType.DMA((5,)),
+            pltpu.SemaphoreType.DMA((len(consts),)),
             pltpu.VMEM((parts, 64 * local, 128), f32),
             pltpu.VMEM((ROWS, 128), f32),
             pltpu.VMEM((ROWS, 128), f32),

time: 45.8 us -> 42.2 us (0.921)
  the two profiles are of different devices: /device:TPU:2 before, /device:TPU:1 now
where the time goes in v1:
time: 42.2 us; the launch traced here: 41.5 us
  Pallas kernels  37.7 us (89%)
  local copies, waits for them, and re-layouts  3.09 us (7%)
  between operations  0.66 us (2%)
    pallas_call x1, Pallas kernels, shards(): pl.pallas_call(functools.partial(body, strips, parts, local), out_shape=j...  37.7 us
    unnamed x2, local copies, waits for them, and re-layouts  3.09 us

profile of v1, /device:TPU:1, one launch (start us, length us, event | category | flops | bytes accessed | tf_op | source)
XLA Modules:
  0.0 41.5 jit_solution(9367332428914445070)
XLA Ops:
  0.7 1.6 %copy.17.kern_ref = f32[3,2,61,61]{3,2,1,0:T(8,128)} copy(f32[3,2,61,61]{3,1,2,0:T(2,128)} %param.18) | data formatting | bytes 178608 | tf_op args[2]
  2.3 37.7 %shard_map.154 = f32[16,1024]{1,0:T(8,128)} custom-call(f32[128,1024]{1,0:T(8,128)} %mask_ref.1, s32[128,1024]{1,0:T(8,128)} %target_ref.1, f32[3,2,61,61]{3,2,1,0:T(8,128)} %copy.17.kern_ref, f32[3]{0:T(128)} %weight_ref.1, s32[1,2]{1,0:T(1,128)} %list_ref.1, s32[1]{0:T(128)S(6)} %copy.19.count_ref, bf16[160,384]{1,0:T(8,128)(2,1)} %constant.20.clone.rest_0_, ...), custom_call_target="tpu_custom_call" | custom-call | tf_op jit(solution)/shard_map/pallas_call | solution.py:400
  40.0 1.5 %copy.20 = f32[16,1024]{1,0:T(8,128)} copy(f32[16,1024]{1,0:T(8,128)} %shard_map.154) | data formatting | bytes 131072

commit v2 on v1

--- a/solution.py
+++ b/solution.py
@@ -60,19 +60,14 @@
     tap_cols[:SUP] = np.concatenate([c, s], 1)
     tc_hi, tc_lo = split_np(tap_cols)
     zero = np.zeros_like(tc_hi)
-
-    def pair(t):
-        return np.concatenate(
-            [np.concatenate([t, zero], 1), np.concatenate([zero, t], 1)], 0
-        )
-
-    tap_col = np.concatenate([pair(tc_hi), pair(tc_hi), pair(tc_lo)], 0)
+    tap_real = np.concatenate([tc_hi, tc_hi, tc_lo, zero], 0)
+    tap_imag = np.concatenate([tc_hi, tc_hi, zero, tc_lo], 0)
     c, s = phases(fr, taps, PERIOD_R)
     tap_rows = np.zeros((2 * FREQ_R, 64))
     tap_rows[:, :SUP] = np.concatenate([c, s], 0)
     tr_hi, tr_lo = split_np(tap_rows)
     tap_row = np.concatenate([tr_hi, tr_hi, tr_lo], 1)
-    return (row_forward, row_back, col_hi, col_lo, inv_hi, inv_lo, inv_mid, src_hi, tap_col, tap_row)
+    return (row_forward, row_back, col_hi, col_lo, inv_hi, inv_lo, inv_mid, src_hi, tap_real, tap_imag, tap_row)
 
 
 def split(value):
@@ -121,9 +116,9 @@
 def run(
     strips, parts, local,
     mask_ref, target_ref, kern_ref, weight_ref, list_ref, count_ref, in_hbm, out_ref, held,
-    raw, mwin, twin, l_sem, t_sem,
+    zbuf, sbuf, raw, mwin, twin, l_sem, t_sem,
     kbuf, halo_src, halo_left, halo_right, xspec, spec, fields, inten, gspec, gwin, rbuf, edge_left, edge_right, acc,
-    k_send, k_recv, h_send, h_recv, g_send, g_recv, e_send, e_recv,
+    k_send, k_recv, r_send, r_recv, h_send, h_recv, g_send, g_recv, e_send, e_recv,
 ):
     t = lax.axis_index("tile")
     j = lax.axis_index("kern")
@@ -133,7 +128,7 @@
     first, last = j == 0, j == parts - 1
     has_up, has_down = t < strips - 1, t > 0
     sends_up, sends_down = last & has_up, first & has_down
-    row_forward, row_back, col_hi, col_lo, inv_hi, inv_lo, inv_mid, src_tab, tap_col, tap_row = held
+    row_forward, row_back, col_hi, col_lo, inv_hi, inv_lo, inv_mid, src_tab, tap_real, tap_imag, tap_row = held
 
     def strip_column(ref, index):
         return ref.at[:, pl.ds(pl.multiple_of(index * 128, 128), 128)]
@@ -158,6 +153,8 @@
     for d in range(1, parts):
         pl.semaphore_signal(barrier, inc=1, device_id=(t, lax.rem(j + d, parts)), device_id_type=MESH)
 
+    pl.semaphore_signal(barrier, inc=1, device_id=(t + 1 - 2 * lax.rem(t, 2), j), device_id_type=MESH)
+
     @pl.when(has_up)
     def _():
         pl.semaphore_signal(barrier, inc=1, device_id=(up, 0), device_id_type=MESH)
@@ -169,8 +166,8 @@
     kbuf[0] = jnp.zeros_like(kbuf[0])
     kern_load.wait()
     for k in range(local):
-        kbuf[0, 64 * k : 64 * k + SUP, 0:SUP] = raw[k, 0]
-        kbuf[0, 64 * k : 64 * k + SUP, 64 : 64 + SUP] = raw[k, 1]
+        kbuf[0, 64 * k : 64 * k + SUP, 0:SUP] = raw[k, :, 0, :]
+        kbuf[0, 64 * k : 64 * k + SUP, 64 : 64 + SUP] = raw[k, :, 1, :]
         kbuf[0, 64 * k + SUP : 64 * k + SUP + 1, :] = jnp.full((1, 128), weight_ref[k], jnp.float32)
 
     def flag(slot):
@@ -194,11 +191,11 @@
 
     @pl.when(edge_device)
     def _():
-        pl.semaphore_wait(barrier, 2 * parts - 1)
+        pl.semaphore_wait(barrier, 2 * parts)
 
     @pl.when(jnp.logical_not(edge_device))
     def _():
-        pl.semaphore_wait(barrier, parts - 1)
+        pl.semaphore_wait(barrier, parts)
 
     def to_down():
         return pltpu.make_async_remote_copy(
@@ -218,14 +215,58 @@
     def _():
         to_up().start()
 
+    core = lax.rem(t, 2)
+    share = 32 * local
+    own_half = pl.ds(pl.multiple_of(core * share, share), share)
+
     def kern_copy(d):
         return pltpu.make_async_remote_copy(
-            kbuf.at[0], kbuf.at[d], k_send.at[d], k_recv.at[d],
+            kbuf.at[0, own_half, :], kbuf.at[d, own_half, :], k_send.at[d], k_recv.at[d],
             device_id=(t, lax.rem(j + d, parts)), device_id_type=MESH)
+
+    def relay(d):
+        return pltpu.make_async_remote_copy(
+            kbuf.at[d, own_half, :], kbuf.at[d, own_half, :], r_send.at[d], r_recv.at[d],
+            device_id=(t + 1 - 2 * core, j), device_id_type=MESH)
 
     for d in range(1, parts):
         kern_copy(d).start()
 
+    inten[...] = jnp.zeros_like(inten)
+
+    for load in table_loads:
+        load.wait()
+    low_lanes = lax.broadcasted_iota(jnp.int32, (2 * FREQ_R, 128), 1) < 64
+
+    def spectra(d):
+        kernels = stacked(jnp.concatenate([kbuf[d, 64 * k : 64 * k + 64, :] for k in range(local)], 1))
+        by_rows = dot(tap_row[...], kernels)
+        for k in range(local):
+            place = d * local + k
+            taken = by_rows[:, 128 * k : 128 * k + 128]
+            high = taken.astype(jnp.bfloat16)
+            high_wide = high.astype(jnp.float32)
+            low = taken - high_wide
+            real = jnp.where(low_lanes, high_wide, pltpu.roll(low, 64, 1)).astype(jnp.bfloat16)
+            imag = jnp.where(low_lanes, pltpu.roll(high_wide, 64, 1), low).astype(jnp.bfloat16)
+            for part, (own, table) in enumerate(((real, tap_real), (imag, tap_imag))):
+                lanes = slice(part * 128, part * 128 + 128)
+                pieces = quarters(dot(jnp.concatenate([own, high], 1), table[...]))
+                for i, piece in enumerate(pieces):
+                    spec[place, i, :, lanes] = piece
+
+    def arrive(d):
+        @pl.when(d + 1 < parts)
+        def _():
+            kern_copy(d + 1).wait_recv()
+            relay(d + 1).start()
+
+        relay(d).wait_recv()
+
+    spectra(0)
+    kern_copy(1).wait_recv()
+    relay(1).start()
+
     @pl.when(sends_down)
     def _():
         to_down().wait()
@@ -236,55 +277,61 @@
 
     before = jnp.where(first, jnp.where(has_down, halo_left[...], 0.0), mwin[0] * live_rows)
     after = jnp.where(last, jnp.where(has_up, halo_right[...], 0.0), mwin[2] * live_rows)
-    for load in table_loads:
-        load.wait()
     window = jnp.concatenate([before[:, SIDE:], here, after[:, :SIDE]], 1)
     by_rows = dot(row_forward[...], stacked(window))
     spectrum = dot3(by_rows, col_hi[...], col_lo[...])
     for place, piece in enumerate(quarters(spectrum)):
         xspec[place] = piece
 
-    inten[...] = jnp.zeros_like(inten)
+    def weight_of(d, k):
+        return kbuf[d, 64 * k + SUP : 64 * k + SUP + 1, :]
+
+    def field_start(d, k, slot):
+        products = []
+        for part in range(2):
+            lanes = slice(part * 128, part * 128 + 128)
+            ur, ui, vr, vi = (spec[d * local + k, i, :, lanes] for i in range(4))
+            xur, xui, xvr, xvi = (xspec[i] for i in range(4))
+            products.append(
+                unquarters(
+                    ur * xur - ui * xui, ur * xui + ui * xur,
+                    vr * xvr - vi * xvi, vr * xvi + vi * xvr,
+                )
+            )
+        y_hi, y_lo = split(jnp.concatenate(products, 0))
+        wide = dot(y_hi, inv_mid[...])
+        inner = wide[:, :128] + (wide[:, 128:] + dot(y_lo, inv_mid[:, :128]))
+        n = 2 * FREQ_R
+        zbuf[slot, k] = stacked(jnp.concatenate([inner[:n], inner[n:]], 1))
+
+    def field_end(d, k, slot):
+        field = dot(row_back[...], zbuf[slot, k])
+        fields[d * local + k] = field
+        real, imag = field[:, :128], field[:, 128:]
+        inten[...] += weight_of(d, k) * (real * real + imag * imag)
+
+    def starts(d):
+        for k in range(local):
+            field_start(d, k, d % 2)
+
+    def ends(d):
+        for k in range(local):
+            field_end(d, k, d % 2)
 
     def forward(d, carry):
-        @pl.when(d > 0)
-        def _():
-            kern_copy(d).wait()
-
-        k_hi, k_lo = split(kbuf[d])
-        taps = dot(jnp.concatenate([k_hi, k_lo], 1), tap_col[0:256, :]) + dot(k_hi, tap_col[256:384, :])
-        t_hi, t_lo = split(taps)
-        for k in range(local):
-            place = d * local + k
-            rows = slice(64 * k, 64 * k + 64)
-            both = dot(tap_row[...], jnp.concatenate([t_hi[rows], t_lo[rows], t_hi[rows]], 0))
-            products = []
-            for part in range(2):
-                lanes = slice(part * 128, part * 128 + 128)
-                ur, ui, vr, vi = quarters(both[:, part * 256 : part * 256 + 256])
-                spec[place, 0, :, lanes] = ur
-                spec[place, 1, :, lanes] = ui
-                spec[place, 2, :, lanes] = vr
-                spec[place, 3, :, lanes] = vi
-                xur, xui, xvr, xvi = xspec[0], xspec[1], xspec[2], xspec[3]
-                products.append(
-                    unquarters(
-                        ur * xur - ui * xui, ur * xui + ui * xur,
-                        vr * xvr - vi * xvi, vr * xvi + vi * xvr,
-                    )
-                )
-            y_hi, y_lo = split(jnp.concatenate(products, 0))
-            wide = dot(y_hi, inv_mid[...])
-            inner = wide[:, :128] + (wide[:, 128:] + dot(y_lo, inv_mid[:, :128]))
-            n = 2 * FREQ_R
-            field = dot(row_back[...], stacked(jnp.concatenate([inner[:n], inner[n:]], 1)))
-            fields[place] = field
-            weight = kbuf[d, 64 * k + SUP : 64 * k + SUP + 1, :]
-            real, imag = field[:, :128], field[:, 128:]
-            inten[...] += weight * (real * real + imag * imag)
+        arrive(d)
+        ends(d - 2)
+        starts(d - 1)
+        spectra(d)
         return carry
 
-    lax.fori_loop(0, parts, forward, 0)
+    arrive(1)
+    starts(0)
+    spectra(1)
+    lax.fori_loop(2, parts, forward, 0)
+    ends(parts - 2)
+    starts(parts - 1)
+    ends(parts - 1)
 
     printed = jax.nn.sigmoid(steepness * (inten[...] - threshold))
     loads[3].wait()
@@ -292,29 +339,41 @@
     inten[...] = live_rows * (4.0 * steepness) * (printed - target) * printed * (1.0 - printed)
     gspec[...] = jnp.zeros_like(gspec)
 
+    def adjoint_start(d, k, slot):
+        slope = inten[...] * weight_of(d, k)
+        source = fields[d * local + k] * jnp.concatenate([slope, slope], 1)
+        by_rows = dot(row_forward[...], stacked(source))
+        hi, lo = split(jnp.concatenate([by_rows[:, :128], by_rows[:, 128:]], 0))
+        sbuf[slot, k, :, 0:128] = hi
+        sbuf[slot, k, :, 128:256] = lo
+
+    def adjoint_end(d, k, slot):
+        found = dot(sbuf[slot, k], src_tab[0:256, :]) + dot(sbuf[slot, k, :, 0:128], src_tab[256:384, :])
+        n = 2 * FREQ_R
+        sums = [0.0] * 4
+        for part in range(2):
+            lanes = slice(part * 128, part * 128 + 128)
+            sur, sui, svr, svi = quarters(found[part * n : part * n + n])
+            ur, ui, vr, vi = (spec[d * local + k, i, :, lanes] for i in range(4))
+            sums[0] += sur * ur + sui * ui
+            sums[1] += sui * ur - sur * ui
+            sums[2] += svr * vr + svi * vi
+            sums[3] += svi * vr - svr * vi
+        for i in range(4):
+            gspec[i] += sums[i]
+
     def adjoint(d, carry):
         for k in range(local):
-            place = d * local + k
-            weight = kbuf[d, 64 * k + SUP : 64 * k + SUP + 1, :]
-            slope = inten[...] * weight
-            source = fields[place] * jnp.concatenate([slope, slope], 1)
-            by_rows = dot(row_forward[...], stacked(source))
-            pair = jnp.concatenate([by_rows[:, :128], by_rows[:, 128:]], 0)
-            s_hi, s_lo = split(pair)
-            found = dot(jnp.concatenate([s_hi, s_lo], 1), src_tab[0:256, :]) + dot(s_hi, src_tab[256:384, :])
-            n = 2 * FREQ_R
-            for part in range(2):
-                lanes = slice(part * 128, part * 128 + 128)
-                sur, sui, svr, svi = quarters(found[part * n : part * n + n])
-                ur, ui = spec[place, 0, :, lanes], spec[place, 1, :, lanes]
-                vr, vi = spec[place, 2, :, lanes], spec[place, 3, :, lanes]
-                gspec[0] += sur * ur + sui * ui
-                gspec[1] += sui * ur - sur * ui
-                gspec[2] += svr * vr + svi * vi
-                gspec[3] += svi * vr - svr * vi
+            adjoint_end(d - 1, k, (d - 1) % 2)
+        for k in range(local):
+            adjoint_start(d, k, d % 2)
         return carry
 
-    lax.fori_loop(0, parts, adjoint, 0)
+    for k in range(local):
+        adjoint_start(0, k, 0)
+    lax.fori_loop(1, parts, adjoint, 0)
+    for k in range(local):
+        adjoint_end(parts - 1, k, (parts - 1) % 2)
 
     total = unquarters(gspec[0], gspec[1], gspec[2], gspec[3])
     inner = dot3(total, inv_hi[...], inv_lo[...])
@@ -374,6 +433,8 @@
     out_ref[...] = acc[:, SIDE : SIDE + BLOCK * parts] * mine
 
     for d in range(1, parts):
+        kern_copy(d).wait_send()
+        relay(d).wait_send()
         grad_copy(d).wait_send()
 
     @pl.when(sends_down)
@@ -397,6 +458,7 @@
     f32 = jnp.float32
     chunk = ROWS // parts
     consts = tables()
+    kernels = jnp.transpose(kernels, (0, 2, 1, 3))
     return pl.pallas_call(
         functools.partial(body, strips, parts, local),
         out_shape=jax.ShapeDtypeStruct((chunk, BLOCK * parts), f32),
@@ -404,6 +466,8 @@
         out_specs=vmem,
         scratch_shapes=[pltpu.VMEM(c.shape, jnp.bfloat16) for c in consts]
         + [
+            pltpu.VMEM((2, local, 6 * FREQ_R, 256), jnp.bfloat16),
+            pltpu.VMEM((2, local, 4 * FREQ_R, 256), jnp.bfloat16),
             pltpu.VMEM(kernels.shape, f32),
             pltpu.VMEM((3, ROWS, 128), f32),
             pltpu.VMEM((ROWS, 128), jnp.int32),
@@ -425,6 +489,8 @@
             pltpu.VMEM((chunk, BLOCK * parts + 128), f32),
             pltpu.SemaphoreType.DMA((parts,)),
             pltpu.SemaphoreType.DMA((parts,)),
+            pltpu.SemaphoreType.DMA((parts,)),
+            pltpu.SemaphoreType.DMA((parts,)),
             pltpu.SemaphoreType.DMA((1,)),
             pltpu.SemaphoreType.DMA((1,)),
             pltpu.SemaphoreType.DMA((parts,)),

time: 42.2 us -> 35 us (0.83)
  the two profiles are of different devices: /device:TPU:1 before, /device:TPU:133 now
where the time goes in v2:
time: 35 us; the launch traced here: 34.8 us
  Pallas kernels  32.7 us (93%)
  local copies, waits for them, and re-layouts  1.47 us (4%)
  between operations  0.66 us (2%)
    pallas_call x1, Pallas kernels, shards(): pl.pallas_call(functools.partial(body, strips, parts, local), out_shape=j...  32.7 us
    unnamed x1, local copies, waits for them, and re-layouts  1.47 us

profile of v2, /device:TPU:133, one launch (start us, length us, event | category | flops | bytes accessed | tf_op | source)
XLA Modules:
  0.0 34.8 jit_solution(8215149221970568659)
XLA Ops:
  0.7 32.7 %shard_map.163 = f32[16,1024]{1,0:T(8,128)} custom-call(f32[128,1024]{1,0:T(8,128)} %mask_ref.1, s32[128,1024]{1,0:T(8,128)} %target_ref.1, f32[3,61,2,61]{3,2,1,0:T(2,128)} %bitcast.1, f32[3]{0:T(128)} %weight_ref.1, s32[1,2]{1,0:T(1,128)} %list_ref.1, s32[1]{0:T(128)S(6)} %copy.19.count_ref, bf16[160,384]{1,0:T(8,128)(2,1)} %constant.22.clone.rest_0_, ...), custom_call_target="tpu_custom_call" | custom-call | tf_op jit(solution)/shard_map/pallas_call | solution.py:462
  33.3 1.5 %copy.20 = f32[16,1024]{1,0:T(8,128)} copy(f32[16,1024]{1,0:T(8,128)} %shard_map.163) | data formatting | bytes 131072

commit v3 on v1

v3 whole, which is shorter than its diff:
```python
import functools

import jax
import jax.numpy as jnp
import ml_dtypes
import numpy as np
from jax import lax
from jax.experimental import pallas as pl
from jax.experimental.pallas import tpu as pltpu
from jax.sharding import PartitionSpec as P

MESH = pl.DeviceIdType.MESH
steepness = 4.0
threshold = 0.6

ROWS = 128
BLOCK = 128
RIM = 30
SUP = 61
PERIOD_R = 159
FREQ_R = 80
PERIOD_C = 255
FREQ_C = 128
SIDE = 64


def split_np(table):
    hi = table.astype(np.float32).astype(ml_dtypes.bfloat16)
    lo = (table - hi.astype(np.float64)).astype(np.float32).astype(ml_dtypes.bfloat16)
    return hi, lo


def phases(first, second, period):
    angle = 2.0 * np.pi / period * (np.outer(first, second) % period)
    return np.cos(angle), np.sin(angle)


@functools.cache
def tables():
    fr, fc = np.arange(FREQ_R), np.arange(FREQ_C)
    rows, window = np.arange(ROWS), np.arange(2 * BLOCK)
    taps = np.arange(SUP) - RIM
    row_weight = np.where(fr == 0, 1.0, 2.0) / PERIOD_R
    col_weight = np.where(fc == 0, 1.0, 2.0) / PERIOD_C * 0.5
    c, s = phases(fr, rows, PERIOD_R)
    to_rows_hi, to_rows_lo = split_np(np.concatenate([c, s], 0))
    row_forward = np.concatenate([to_rows_hi, to_rows_hi, to_rows_lo], 1)
    back = np.concatenate([c * row_weight[:, None], s * row_weight[:, None]], 0).T
    back_hi, back_lo = split_np(back)
    row_back = np.concatenate([back_hi, back_hi, back_lo], 1)
    c, s = phases(window, fc, PERIOD_C)
    col_hi, col_lo = split_np(np.concatenate([c, s], 1))
    inv = np.concatenate([(c * col_weight).T, (s * col_weight).T], 0)
    inv_hi, inv_lo = split_np(inv)
    mid = slice(SIDE, SIDE + BLOCK)
    inv_mid = np.concatenate([inv_hi[:, mid], inv_lo[:, mid]], 1)
    src_hi = np.concatenate([col_hi[mid], col_hi[mid], col_lo[mid]], 0)
    c, s = phases(taps, fc, PERIOD_C)
    tap_cols = np.zeros((64, 2 * FREQ_C))
    tap_cols[:SUP] = np.concatenate([c, s], 1)
    tc_hi, tc_lo = split_np(tap_cols)
    zero = np.zeros_like(tc_hi)
    tap_real = np.concatenate([tc_hi, tc_hi, tc_lo, zero], 0)
    tap_imag = np.concatenate([tc_hi, tc_hi, zero, tc_lo], 0)
    c, s = phases(fr, taps, PERIOD_R)
    tap_rows = np.zeros((2 * FREQ_R, 64))
    tap_rows[:, :SUP] = np.concatenate([c, s], 0)
    tr_hi, tr_lo = split_np(tap_rows)
    tap_row = np.concatenate([tr_hi, tr_hi, tr_lo], 1)
    return (row_forward, row_back, col_hi, col_lo, inv_hi, inv_lo, inv_mid, src_hi, tap_real, tap_imag, tap_row)


def split(value):
    hi = value.astype(jnp.bfloat16)
    lo = (value - hi.astype(jnp.float32)).astype(jnp.bfloat16)
    return hi, lo


def dot(a, b):
    return jnp.dot(a, b, preferred_element_type=jnp.float32)


def dot3(a, b_hi, b_lo):
    a_hi, a_lo = split(a)
    return dot(a_hi, b_hi) + (dot(a_lo, b_hi) + dot(a_hi, b_lo))


def stacked(value):
    hi, lo = split(value)
    return jnp.concatenate([hi, lo, hi], 0)


def quarters(spec):
    cc, cs = spec[:FREQ_R, :FREQ_C], spec[:FREQ_R, FREQ_C:]
    sc, ss = spec[FREQ_R:, :FREQ_C], spec[FREQ_R:, FREQ_C:]
    return cc - ss, cs + sc, cc + ss, sc - cs


def unquarters(ur, ui, vr, vi):
    top = jnp.concatenate([ur + vr, ui - vi], 1)
    bottom = jnp.concatenate([ui + vi, vr - ur], 1)
    return jnp.concatenate([top, bottom], 0)


def body(
    strips, parts, local,
    mask_ref, target_ref, kern_ref, weight_ref, list_ref, count_ref, *rest,
):
    table_count = len(tables())
    in_hbm, rest = rest[:table_count], rest[table_count:]
    out_ref, rest = rest[0], rest[1:]
    held, rest = rest[:table_count], rest[table_count:]
    run(strips, parts, local, mask_ref, target_ref, kern_ref, weight_ref, list_ref, count_ref, in_hbm, out_ref, held, *rest)


def run(
    strips, parts, local,
    mask_ref, target_ref, kern_ref, weight_ref, list_ref, count_ref, in_hbm, out_ref, held,
    zbuf, sbuf, raw, mwin, twin, l_sem, t_sem,
    kbuf, halo_src, halo_left, halo_right, xspec, spec, fields, inten, other, slope, gspec, gwin, rbuf,
    edge_left, edge_right, acc,
    ready, k_send, k_recv, h_send, h_recv, p_send, p_recv, g_send, g_recv, e_send, e_recv,
):
    t = lax.axis_index("tile")
    j = lax.axis_index("kern")
    up = lax.rem(t + 1, strips)
    down = lax.rem(t + strips - 1, strips)
    chunk = ROWS // parts
    groups = parts // 2

    def columns_of(device):
        return 2 * lax.rem((device // 2 + 1) // 2, 2) + lax.rem(device, 2)

    def device_of(half, columns):
        inner = columns // 2
        return 2 * (inner + half * (3 - 2 * inner)) + lax.rem(columns, 2)

    mine_half, x = j // 4, columns_of(j)
    first, last = x == 0, x == groups - 1
    has_up, has_down = t < strips - 1, t > 0
    sends_up, sends_down = last & has_up, first & has_down
    left_end, right_end = device_of(mine_half, 0), device_of(mine_half, groups - 1)
    row_forward, row_back, col_hi, col_lo, inv_hi, inv_lo, inv_mid, src_tab, tap_real, tap_imag, tap_row = held

    def strip_column(ref, index):
        return ref.at[:, pl.ds(pl.multiple_of(index * 128, 128), 128)]

    def block_at(group, turn):
        return jnp.where(group == 0, 1 - turn, turn)

    kern_load = pltpu.make_async_copy(kern_ref, raw, l_sem.at[0])
    kern_load.start()
    at = 2 * x
    places = (jnp.maximum(at - 1, 0), at, at + 1, jnp.minimum(at + 2, parts - 1))
    loads = [
        pltpu.make_async_copy(strip_column(mask_ref, place), mwin.at[i], l_sem.at[1 + i])
        for i, place in enumerate(places)
    ]
    target_loads = [
        pltpu.make_async_copy(strip_column(target_ref, at + block_at(x, b)), twin.at[b], l_sem.at[5 + b])
        for b in range(2)
    ]
    table_loads = [
        pltpu.make_async_copy(source, place, t_sem.at[i]) for i, (source, place) in enumerate(zip(in_hbm, held))
    ]
    for load in loads + table_loads + target_loads:
        load.start()

    barrier = pltpu.get_barrier_semaphore()
    for d in range(1, parts):
        pl.semaphore_signal(barrier, inc=1, device_id=(t, lax.rem(j + d, parts)), device_id_type=MESH)

    @pl.when(sends_up)
    def _():
        pl.semaphore_signal(barrier, inc=1, device_id=(up, left_end), device_id_type=MESH)

    @pl.when(sends_down)
    def _():
        pl.semaphore_signal(barrier, inc=1, device_id=(down, right_end), device_id_type=MESH)

    kbuf[0] = jnp.zeros_like(kbuf[0])
    kern_load.wait()
    for k in range(local):
        kbuf[0, 64 * k : 64 * k + SUP, 0:SUP] = raw[k, :, 0, :]
        kbuf[0, 64 * k : 64 * k + SUP, 64 : 64 + SUP] = raw[k, :, 1, :]
        kbuf[0, 64 * k + SUP : 64 * k + SUP + 1, :] = jnp.full((1, 128), weight_ref[k], jnp.float32)

    def flag(slot):
        found = jnp.float32(0.0)
        for place in range(2):
            hit = (list_ref[0, place] == slot) & (place < count_ref[0])
            found = jnp.where(hit, jnp.float32(1.0), found)
        return found

    half = ROWS // 2
    live_rows = jnp.concatenate(
        [jnp.full((half, 128), flag(0), jnp.float32), jnp.full((half, 128), flag(1), jnp.float32)], 0
    )

    for load in loads:
        load.wait()
    halo_src[...] = jnp.where(first, mwin[1], mwin[2]) * live_rows

    edge_device = sends_up | sends_down

    @pl.when(edge_device)
    def _():
        pl.semaphore_wait(barrier, parts)

    @pl.when(jnp.logical_not(edge_device))
    def _():
        pl.semaphore_wait(barrier, parts - 1)

    def to_down():
        return pltpu.make_async_remote_copy(
            halo_src, halo_right, h_send.at[0], h_recv.at[0],
            device_id=(down, right_end), device_id_type=MESH)

    def to_up():
        return pltpu.make_async_remote_copy(
            halo_src, halo_left, h_send.at[0], h_recv.at[0],
            device_id=(up, left_end), device_id_type=MESH)

    @pl.when(sends_down)
    def _():
        to_down().start()
        pl.semaphore_signal(ready, inc=1, device_id=(down, right_end), device_id_type=MESH)

    @pl.when(sends_up)
    def _():
        to_up().start()
        pl.semaphore_signal(ready, inc=1, device_id=(up, left_end), device_id_type=MESH)

    x_hi, x_lo = x // 2, lax.rem(x, 2)
    peers = [x, 2 * (1 - x_hi) + x_lo, 2 * x_hi + 1 - x_lo, 2 * (1 - x_hi) + 1 - x_lo]

    def kern_copy(slot, peer=peers[1]):
        return pltpu.make_async_remote_copy(
            kbuf.at[0], kbuf.at[slot], k_send.at[slot], k_recv.at[slot],
            device_id=(t, device_of(mine_half, peer)), device_id_type=MESH)

    for slot in range(1, groups):
        kern_copy(slot, peers[slot]).start()

    for load in table_loads:
        load.wait()
    low_lanes = lax.broadcasted_iota(jnp.int32, (2 * FREQ_R, 128), 1) < 64

    def spectra(e):
        kernels = stacked(jnp.concatenate([kbuf[e, 64 * k : 64 * k + 64, :] for k in range(local)], 1))
        by_rows = dot(tap_row[...], kernels)
        for k in range(local):
            place = e * local + k
            taken = by_rows[:, 128 * k : 128 * k + 128]
            high = taken.astype(jnp.bfloat16)
            high_wide = high.astype(jnp.float32)
            low = taken - high_wide
            real = jnp.where(low_lanes, high_wide, pltpu.roll(low, 64, 1)).astype(jnp.bfloat16)
            imag = jnp.where(low_lanes, pltpu.roll(high_wide, 64, 1), low).astype(jnp.bfloat16)
            for part, (own, table) in enumerate(((real, tap_real), (imag, tap_imag))):
                lanes = slice(part * 128, part * 128 + 128)
                pieces = quarters(dot(jnp.concatenate([own, high], 1), table[...]))
                for i, piece in enumerate(pieces):
                    spec[place, i, :, lanes] = piece

    def weight_of(e, k):
        return kbuf[e, 64 * k + SUP : 64 * k + SUP + 1, :]

    def starts(e, b):
        n = 2 * FREQ_R
        for k in range(local):
            products = []
            for part in range(2):
                lanes = slice(part * 128, part * 128 + 128)
                ur, ui, vr, vi = (spec[e * local + k, i, :, lanes] for i in range(4))
                xur, xui, xvr, xvi = (xspec[b, i] for i in range(4))
                products.append(
                    unquarters(
                        ur * xur - ui * xui, ur * xui + ui * xur,
                        vr * xvr - vi * xvi, vr * xvi + vi * xvr,
                    )
                )
            y_hi, y_lo = split(jnp.concatenate(products, 0))
            wide = dot(y_hi, inv_mid[...])
            inner = wide[:, :128] + (wide[:, 128:] + dot(y_lo, inv_mid[:, :128]))
            zbuf[b, k] = stacked(jnp.concatenate([inner[:n], inner[n:]], 1))

    def ends(e, b):
        for k in range(local):
            field = dot(row_back[...], zbuf[b, k])
            fields[b, e * local + k] = field
            real, imag = field[:, :128], field[:, 128:]
            inten[b] += weight_of(e, k) * (real * real + imag * imag)

    spectra(0)

    pair = [mwin[1] * live_rows, mwin[2] * live_rows]

    def transform(b, window):
        by_rows = dot(row_forward[...], stacked(window))
        spectrum = dot3(by_rows, col_hi[...], col_lo[...])
        for i, piece in enumerate(quarters(spectrum)):
            xspec[b, i] = piece

    before, after = mwin[0] * live_rows, mwin[3] * live_rows
    left = jnp.concatenate([before[:, SIDE:], pair[0], pair[1][:, :SIDE]], 1)
    right = jnp.concatenate([pair[0][:, SIDE:], pair[1], after[:, :SIDE]], 1)
    transform(0, jnp.where(first, right, left))
    inten[...] = jnp.zeros_like(inten)

    def forward(e, carry):
        ends(e - 1, 0)
        kern_copy(e).wait_recv()
        spectra(e)
        starts(e, 0)
        return carry

    def second(e, carry):
        ends(e - 1, 1)
        starts(e, 1)
        return carry

    def swap(b):
        return pltpu.make_async_remote_copy(
            inten.at[b], other.at[b], p_send.at[b], p_recv.at[b],
            device_id=(t, device_of(1 - mine_half, x)), device_id_type=MESH)

    starts(0, 0)
    lax.fori_loop(1, groups, forward, 0)
    ends(groups - 1, 0)
    swap(0).start()

    @pl.when(sends_down)
    def _():
        to_down().wait()

    @pl.when(sends_up)
    def _():
        to_up().wait()

    before = jnp.where(has_down, halo_left[...], 0.0)
    after = jnp.where(last, jnp.where(has_up, halo_right[...], 0.0), mwin[3] * live_rows)
    left = jnp.concatenate([before[:, SIDE:], pair[0], pair[1][:, :SIDE]], 1)
    right = jnp.concatenate([pair[0][:, SIDE:], pair[1], after[:, :SIDE]], 1)
    transform(1, jnp.where(first, left, right))
    starts(0, 1)
    lax.fori_loop(1, groups, second, 0)
    ends(groups - 1, 1)
    swap(1).start()
    gspec[...] = jnp.zeros_like(gspec)

    def slope_of(b):
        target_loads[b].wait()
        swap(b).wait_recv()
        printed = jax.nn.sigmoid(steepness * (inten[b] + other[b] - threshold))
        target = twin[b].astype(jnp.float32)
        slope[b] = live_rows * (4.0 * steepness) * (printed - target) * printed * (1.0 - printed)

    def adjoint_start(e, b, slot):
        for k in range(local):
            tilt = slope[b] * weight_of(e, k)
            source = fields[b, e * local + k] * jnp.concatenate([tilt, tilt], 1)
            by_rows = dot(row_forward[...], stacked(source))
            hi, lo = split(jnp.concatenate([by_rows[:, :128], by_rows[:, 128:]], 0))
            sbuf[slot, k, :, 0:128] = hi
            sbuf[slot, k, :, 128:256] = lo

    def adjoint_end(e, b, slot):
        n = 2 * FREQ_R
        for k in range(local):
            found = dot(sbuf[slot, k], src_tab[0:256, :]) + dot(sbuf[slot, k, :, 0:128], src_tab[256:384, :])
            sums = [0.0] * 4
            for part in range(2):
                lanes = slice(part * 128, part * 128 + 128)
                sur, sui, svr, svi = quarters(found[part * n : part * n + n])
                ur, ui, vr, vi = (spec[e * local + k, i, :, lanes] for i in range(4))
                sums[0] += sur * ur + sui * ui
                sums[1] += sui * ur - sur * ui
                sums[2] += svr * vr + svi * vi
                sums[3] += svi * vr - svr * vi
            for i in range(4):
                gspec[b, i] += sums[i]

    def adjoint(b):
        def step(e, carry):
            adjoint_end(e - 1, b, (e - 1) % 2)
            adjoint_start(e, b, e % 2)
            return carry

        return step

    def inverse(b):
        total = unquarters(gspec[b, 0], gspec[b, 1], gspec[b, 2], gspec[b, 3])
        gwin[b] = dot(row_back[...], stacked(dot3(total, inv_hi[...], inv_lo[...])))

    def rows_of(index):
        return pl.ds(pl.multiple_of(index * chunk, chunk), chunk)

    def grad_copy(b, d):
        owner = lax.rem(j + d, parts)
        return pltpu.make_async_remote_copy(
            gwin.at[b, rows_of(owner), :], rbuf.at[b, d], g_send.at[b, d], g_recv.at[b, d],
            device_id=(t, owner), device_id_type=MESH)

    def edge_down(i):
        return pltpu.make_async_remote_copy(
            gwin.at[1, i * chunk : (i + 1) * chunk, 0:128], edge_right.at[mine_half], e_send.at[i], e_recv.at[0, mine_half],
            device_id=(down, i), device_id_type=MESH)

    def edge_up(i):
        return pltpu.make_async_remote_copy(
            gwin.at[1, i * chunk : (i + 1) * chunk, 128:256], edge_left.at[mine_half], e_send.at[i], e_recv.at[1, mine_half],
            device_id=(up, i), device_id_type=MESH)

    end = groups - 1
    slope_of(0)
    adjoint_start(0, 0, 0)
    lax.fori_loop(1, groups, adjoint(0), 0)
    slope_of(1)
    adjoint_end(end, 0, end % 2)
    adjoint_start(0, 1, 0)
    inverse(0)

    for d in range(1, parts):
        grad_copy(0, d).start()
    lax.fori_loop(1, groups, adjoint(1), 0)
    adjoint_end(end, 1, end % 2)
    inverse(1)

    @pl.when(sends_down)
    def _():
        pl.semaphore_wait(ready, 1)
        for i in range(parts):
            edge_down(i).start()

    @pl.when(sends_up)
    def _():
        pl.semaphore_wait(ready, 1)
        for i in range(parts):
            edge_up(i).start()

    for d in range(1, parts):
        grad_copy(1, d).start()

    def span(source, b):
        group = columns_of(source)
        return pl.ds(pl.multiple_of((2 * group + block_at(group, b)) * 128, 128), 256)

    acc[...] = jnp.zeros_like(acc)
    for b in range(2):
        acc[:, span(j, b)] += gwin[b, rows_of(j), :]
        for d in range(1, parts):
            grad_copy(b, d).wait_recv()
            acc[:, span(lax.rem(j + parts - d, parts), b)] += rbuf[b, d]

    @pl.when(has_up)
    def _():
        for side in range(2):
            pltpu.make_async_copy(edge_right.at[side], edge_right.at[side], e_recv.at[0, side]).wait()
        acc[:, BLOCK * parts :] += edge_right[0] + edge_right[1]

    @pl.when(has_down)
    def _():
        for side in range(2):
            pltpu.make_async_copy(edge_left.at[side], edge_left.at[side], e_recv.at[1, side]).wait()
        acc[:, 0:128] += edge_left[0] + edge_left[1]

    mine = jnp.where(j < groups, flag(0), flag(1))
    out_ref[...] = acc[:, SIDE : SIDE + BLOCK * parts] * mine

    for slot in range(1, groups):
        kern_copy(slot).wait_send()
    for b in range(2):
        swap(b).wait_send()
        for d in range(1, parts):
            grad_copy(b, d).wait_send()

    @pl.when(sends_down)
    def _():
        for i in range(parts):
            edge_down(i).wait_send()

    @pl.when(sends_up)
    def _():
        for i in range(parts):
            edge_up(i).wait_send()


def shards(mask_field, target_image, kernels, kernel_weights, live_list, live_count):
    strips, parts = lax.axis_size("tile"), lax.axis_size("kern")
    local = kernels.shape[0]
    groups = parts // 2
    count = local * groups
    vmem = pl.BlockSpec(memory_space=pltpu.VMEM)
    smem = pl.BlockSpec(memory_space=pltpu.SMEM)
    hbm = pl.BlockSpec(memory_space=pl.ANY)
    f32, bf16 = jnp.float32, jnp.bfloat16
    dma = pltpu.SemaphoreType.DMA
    chunk = ROWS // parts
    consts = tables()
    kernels = jnp.transpose(kernels, (0, 2, 1, 3))
    return pl.pallas_call(
        functools.partial(body, strips, parts, local),
        out_shape=jax.ShapeDtypeStruct((chunk, BLOCK * parts), f32),
        in_specs=[hbm, hbm, hbm, smem, smem, smem] + [hbm] * len(consts),
        out_specs=vmem,
        scratch_shapes=[pltpu.VMEM(c.shape, bf16) for c in consts]
        + [
            pltpu.VMEM((2, local, 6 * FREQ_R, 256), bf16),
            pltpu.VMEM((2, local, 4 * FREQ_R, 256), bf16),
            pltpu.VMEM(kernels.shape, f32),
            pltpu.VMEM((4, ROWS, 128), f32),
            pltpu.VMEM((2, ROWS, 128), jnp.int32),
            dma((7,)),
            dma((len(consts),)),
            pltpu.VMEM((groups, 64 * local, 128), f32),
            pltpu.VMEM((ROWS, 128), f32),
            pltpu.VMEM((ROWS, 128), f32),
            pltpu.VMEM((ROWS, 128), f32),
            pltpu.VMEM((2, 4, FREQ_R, FREQ_C), f32),
            pltpu.VMEM((count, 4, FREQ_R, 2 * FREQ_C), f32),
            pltpu.VMEM((2, count, ROWS, 256), f32),
            pltpu.VMEM((2, ROWS, 128), f32),
            pltpu.VMEM((2, ROWS, 128), f32),
            pltpu.VMEM((2, ROWS, 128), f32),
            pltpu.VMEM((2, 4, FREQ_R, FREQ_C), f32),
            pltpu.VMEM((2, ROWS, 256), f32),
            pltpu.VMEM((2, parts, chunk, 256), f32),
            pltpu.VMEM((2, chunk, 128), f32),
            pltpu.VMEM((2, chunk, 128), f32),
            pltpu.VMEM((chunk, BLOCK * parts + 128), f32),
            pltpu.SemaphoreType.REGULAR,
            dma((groups,)),
            dma((groups,)),
            dma((1,)),
            dma((1,)),
            dma((2,)),
            dma((2,)),
            dma((2, parts)),
            dma((2, parts)),
            dma((parts,)),
            dma((2, 2)),
        ],
        compiler_params=pltpu.CompilerParams(
            collective_id=0, has_side_effects=True, vmem_limit_bytes=56 * 1024 * 1024
        ),
    )(mask_field, target_image, kernels, kernel_weights, live_list, live_count, *consts)


def solution(mesh):
    placed = (
        P(None, "tile"),
        P(None, "tile"),
        P("kern", None, None, None),
        P("kern"),
        P("tile", None),
        P("tile"),
    )
    return jax.shard_map(
        shards, mesh=mesh, in_specs=placed, out_specs=P("kern", "tile"), check_vma=False
    )
```

time: 42.2 us -> 33.5 us (0.79); the launches traced: 41.5 us -> 33.3 us
  Pallas kernels: 37.7 us -> 31.2 us
  local copies, waits for them, and re-layouts: 3.09 us -> 1.47 us
    pallas_call x1, Pallas kernels: 37.7 us -> 31.2 us  [shards(): pl.pallas_call(functools.partial(body, strips, parts, local), out_shape=j...]
    unnamed x2 -> x1, local copies, waits for them, and re-layouts: 3.09 us -> 1.47 us
where the time goes in v3:
time: 33.5 us; the launch traced here: 33.3 us
  Pallas kernels  31.2 us (93%)
  local copies, waits for them, and re-layouts  1.47 us (4%)
  between operations  0.66 us (2%)
    pallas_call x1, Pallas kernels, shards(): pl.pallas_call(functools.partial(body, strips, parts, local), out_shape=j...  31.2 us
    unnamed x1, local copies, waits for them, and re-layouts  1.47 us

profile of v3, /device:TPU:1, one launch (start us, length us, event | category | flops | bytes accessed | tf_op | source)
XLA Modules:
  0.0 33.3 jit_solution(1615519995449272880)
XLA Ops:
  0.7 31.2 %shard_map.163 = f32[16,1024]{1,0:T(8,128)} custom-call(f32[128,1024]{1,0:T(8,128)} %mask_ref.1, s32[128,1024]{1,0:T(8,128)} %target_ref.1, f32[3,61,2,61]{3,2,1,0:T(2,128)} %bitcast.1, f32[3]{0:T(128)} %weight_ref.1, s32[1,2]{1,0:T(1,128)} %list_ref.1, s32[1]{0:T(128)S(6)} %copy.19.count_ref, bf16[160,384]{1,0:T(8,128)(2,1)} %constant.22.clone.rest_0_, ...), custom_call_target="tpu_custom_call" | custom-call | tf_op jit(solution)/shard_map/pallas_call | solution.py:502
  31.8 1.5 %copy.20 = f32[16,1024]{1,0:T(8,128)} copy(f32[16,1024]{1,0:T(8,128)} %shard_map.163) | data formatting | bytes 131072

commit v4 on v3

--- a/solution.py
+++ b/solution.py
@@ -150,6 +150,23 @@
 
     kern_load = pltpu.make_async_copy(kern_ref, raw, l_sem.at[0])
     kern_load.start()
+
+    x_hi, x_lo = x // 2, lax.rem(x, 2)
+    peers = [x, 2 * (1 - x_hi) + x_lo, 2 * x_hi + 1 - x_lo, 2 * (1 - x_hi) + 1 - x_lo]
+
+    barrier = pltpu.get_barrier_semaphore()
+    greeted = [device_of(mine_half, peer) for peer in peers[1:]] + [device_of(1 - mine_half, x)]
+    for device in greeted:
+        pl.semaphore_signal(barrier, inc=1, device_id=(t, device), device_id_type=MESH)
+
+    @pl.when(sends_up)
+    def _():
+        pl.semaphore_signal(barrier, inc=1, device_id=(up, left_end), device_id_type=MESH)
+
+    @pl.when(sends_down)
+    def _():
+        pl.semaphore_signal(barrier, inc=1, device_id=(down, right_end), device_id_type=MESH)
+
     at = 2 * x
     places = (jnp.maximum(at - 1, 0), at, at + 1, jnp.minimum(at + 2, parts - 1))
     loads = [
@@ -166,18 +183,6 @@
     for load in loads + table_loads + target_loads:
         load.start()
 
-    barrier = pltpu.get_barrier_semaphore()
-    for d in range(1, parts):
-        pl.semaphore_signal(barrier, inc=1, device_id=(t, lax.rem(j + d, parts)), device_id_type=MESH)
-
-    @pl.when(sends_up)
-    def _():
-        pl.semaphore_signal(barrier, inc=1, device_id=(up, left_end), device_id_type=MESH)
-
-    @pl.when(sends_down)
-    def _():
-        pl.semaphore_signal(barrier, inc=1, device_id=(down, right_end), device_id_type=MESH)
-
     kbuf[0] = jnp.zeros_like(kbuf[0])
     kern_load.wait()
     for k in range(local):
@@ -197,50 +202,45 @@
         [jnp.full((half, 128), flag(0), jnp.float32), jnp.full((half, 128), flag(1), jnp.float32)], 0
     )
 
+    edge_device = sends_up | sends_down
+
+    @pl.when(edge_device)
+    def _():
+        pl.semaphore_wait(barrier, len(greeted) + 1)
+
+    @pl.when(jnp.logical_not(edge_device))
+    def _():
+        pl.semaphore_wait(barrier, len(greeted))
+
+    def to_down():
+        return pltpu.make_async_remote_copy(
+            halo_src, halo_right, h_send.at[0], h_recv.at[0],
+            device_id=(down, right_end), device_id_type=MESH)
+
+    def to_up():
+        return pltpu.make_async_remote_copy(
+            halo_src, halo_left, h_send.at[0], h_recv.at[0],
+            device_id=(up, left_end), device_id_type=MESH)
+
+    def kern_copy(slot, peer=peers[1]):
+        return pltpu.make_async_remote_copy(
+            kbuf.at[0], kbuf.at[slot], k_send.at[slot], k_recv.at[slot],
+            device_id=(t, device_of(mine_half, peer)), device_id_type=MESH)
+
+    for slot in range(1, groups):
+        kern_copy(slot, peers[slot]).start()
+
     for load in loads:
         load.wait()
     halo_src[...] = jnp.where(first, mwin[1], mwin[2]) * live_rows
 
-    edge_device = sends_up | sends_down
-
-    @pl.when(edge_device)
-    def _():
-        pl.semaphore_wait(barrier, parts)
-
-    @pl.when(jnp.logical_not(edge_device))
-    def _():
-        pl.semaphore_wait(barrier, parts - 1)
-
-    def to_down():
-        return pltpu.make_async_remote_copy(
-            halo_src, halo_right, h_send.at[0], h_recv.at[0],
-            device_id=(down, right_end), device_id_type=MESH)
-
-    def to_up():
-        return pltpu.make_async_remote_copy(
-            halo_src, halo_left, h_send.at[0], h_recv.at[0],
-            device_id=(up, left_end), device_id_type=MESH)
-
     @pl.when(sends_down)
     def _():
         to_down().start()
-        pl.semaphore_signal(ready, inc=1, device_id=(down, right_end), device_id_type=MESH)
 
     @pl.when(sends_up)
     def _():
         to_up().start()
-        pl.semaphore_signal(ready, inc=1, device_id=(up, left_end), device_id_type=MESH)
-
-    x_hi, x_lo = x // 2, lax.rem(x, 2)
-    peers = [x, 2 * (1 - x_hi) + x_lo, 2 * x_hi + 1 - x_lo, 2 * (1 - x_hi) + 1 - x_lo]
-
-    def kern_copy(slot, peer=peers[1]):
-        return pltpu.make_async_remote_copy(
-            kbuf.at[0], kbuf.at[slot], k_send.at[slot], k_recv.at[slot],
-            device_id=(t, device_of(mine_half, peer)), device_id_type=MESH)
-
-    for slot in range(1, groups):
-        kern_copy(slot, peers[slot]).start()
 
     for load in table_loads:
         load.wait()
@@ -414,6 +414,15 @@
 
     end = groups - 1
     slope_of(0)
+
+    @pl.when(sends_down)
+    def _():
+        pl.semaphore_signal(ready, inc=1, device_id=(down, right_end), device_id_type=MESH)
+
+    @pl.when(sends_up)
+    def _():
+        pl.semaphore_signal(ready, inc=1, device_id=(up, left_end), device_id_type=MESH)
+
     adjoint_start(0, 0, 0)
     lax.fori_loop(1, groups, adjoint(0), 0)
     slope_of(1)

time: 33.5 us -> 32.5 us (0.970)
  Pallas kernels: 31.2 us -> 30.2 us
    pallas_call x1, Pallas kernels: 31.2 us -> 30.2 us  [shards(): pl.pallas_call(functools.partial(body, strips, parts, local), out_shape=j...]
where the time goes in v4:
time: 32.5 us; the launch traced here: 32.4 us
  Pallas kernels  30.2 us (93%)
  local copies, waits for them, and re-layouts  1.47 us (5%)
  between operations  0.66 us (2%)
    pallas_call x1, Pallas kernels, shards(): pl.pallas_call(functools.partial(body, strips, parts, local), out_shape=j...  30.2 us
    unnamed x1, local copies, waits for them, and re-layouts  1.47 us

profile of v4, /device:TPU:1, one launch (start us, length us, event | category | flops | bytes accessed | tf_op | source)
XLA Modules:
  0.0 32.4 jit_solution(7001853961695957989)
XLA Ops:
  0.7 30.2 %shard_map.163 = f32[16,1024]{1,0:T(8,128)} custom-call(f32[128,1024]{1,0:T(8,128)} %mask_ref.1, s32[128,1024]{1,0:T(8,128)} %target_ref.1, f32[3,61,2,61]{3,2,1,0:T(2,128)} %bitcast.1, f32[3]{0:T(128)} %weight_ref.1, s32[1,2]{1,0:T(1,128)} %list_ref.1, s32[1]{0:T(128)S(6)} %copy.19.count_ref, bf16[160,384]{1,0:T(8,128)(2,1)} %constant.22.clone.rest_0_, ...), custom_call_target="tpu_custom_call" | custom-call | tf_op jit(solution)/shard_map/pallas_call | solution.py:511
  30.9 1.5 %copy.20 = f32[16,1024]{1,0:T(8,128)} copy(f32[16,1024]{1,0:T(8,128)} %shard_map.163) | data formatting | bytes 131072

commit v5 on v4

--- a/solution.py
+++ b/solution.py
@@ -326,7 +326,7 @@
             device_id=(t, device_of(1 - mine_half, x)), device_id_type=MESH)
 
     starts(0, 0)
-    lax.fori_loop(1, groups, forward, 0)
+    lax.fori_loop(1, groups, forward, 0, unroll=True)
     ends(groups - 1, 0)
     swap(0).start()
 
@@ -344,7 +344,7 @@
     right = jnp.concatenate([pair[0][:, SIDE:], pair[1], after[:, :SIDE]], 1)
     transform(1, jnp.where(first, left, right))
     starts(0, 1)
-    lax.fori_loop(1, groups, second, 0)
+    lax.fori_loop(1, groups, second, 0, unroll=True)
     ends(groups - 1, 1)
     swap(1).start()
     gspec[...] = jnp.zeros_like(gspec)
@@ -424,7 +424,7 @@
         pl.semaphore_signal(ready, inc=1, device_id=(up, left_end), device_id_type=MESH)
 
     adjoint_start(0, 0, 0)
-    lax.fori_loop(1, groups, adjoint(0), 0)
+    lax.fori_loop(1, groups, adjoint(0), 0, unroll=True)
     slope_of(1)
     adjoint_end(end, 0, end % 2)
     adjoint_start(0, 1, 0)
@@ -432,7 +432,7 @@
 
     for d in range(1, parts):
         grad_copy(0, d).start()
-    lax.fori_loop(1, groups, adjoint(1), 0)
+    lax.fori_loop(1, groups, adjoint(1), 0, unroll=True)
     adjoint_end(end, 1, end % 2)
     inverse(1)
 

time: 32.5 us -> 31.5 us (0.969)
  Pallas kernels: 30.2 us -> 29.2 us
    pallas_call x1, Pallas kernels: 30.2 us -> 29.2 us  [shards(): pl.pallas_call(functools.partial(body, strips, parts, local), out_shape=j...]
where the time goes in v5:
time: 31.5 us; the launch traced here: 31.4 us
  Pallas kernels  29.2 us (93%)
  local copies, waits for them, and re-layouts  1.47 us (5%)
  between operations  0.66 us (2%)
    pallas_call x1, Pallas kernels, shards(): pl.pallas_call(functools.partial(body, strips, parts, local), out_shape=j...  29.2 us
    unnamed x1, local copies, waits for them, and re-layouts  1.47 us

profile of v5, /device:TPU:1, one launch (start us, length us, event | category | flops | bytes accessed | tf_op | source)
XLA Modules:
  0.0 31.4 jit_solution(11618391380337392886)
XLA Ops:
  0.7 29.2 %shard_map.163 = f32[16,1024]{1,0:T(8,128)} custom-call(f32[128,1024]{1,0:T(8,128)} %mask_ref.1, s32[128,1024]{1,0:T(8,128)} %target_ref.1, f32[3,61,2,61]{3,2,1,0:T(2,128)} %bitcast.1, f32[3]{0:T(128)} %weight_ref.1, s32[1,2]{1,0:T(1,128)} %list_ref.1, s32[1]{0:T(128)S(6)} %copy.19.count_ref, bf16[160,384]{1,0:T(8,128)(2,1)} %constant.22.clone.rest_0_, ...), custom_call_target="tpu_custom_call" | custom-call | tf_op jit(solution)/shard_map/pallas_call | solution.py:511
  29.9 1.5 %copy.20 = f32[16,1024]{1,0:T(8,128)} copy(f32[16,1024]{1,0:T(8,128)} %shard_map.163) | data formatting | bytes 131072

commit v6 on v5

--- a/solution.py
+++ b/solution.py
@@ -242,7 +242,7 @@
     def _():
         to_up().start()
 
-    for load in table_loads:
+    for load in table_loads[8:]:
         load.wait()
     low_lanes = lax.broadcasted_iota(jnp.int32, (2 * FREQ_R, 128), 1) < 64
 
@@ -293,6 +293,8 @@
             inten[b] += weight_of(e, k) * (real * real + imag * imag)
 
     spectra(0)
+    for load in table_loads[:8]:
+        load.wait()
 
     pair = [mwin[1] * live_rows, mwin[2] * live_rows]
 
@@ -436,6 +438,9 @@
     adjoint_end(end, 1, end % 2)
     inverse(1)
 
+    for d in range(1, parts):
+        grad_copy(1, d).start()
+
     @pl.when(sends_down)
     def _():
         pl.semaphore_wait(ready, 1)
@@ -447,9 +452,6 @@
         pl.semaphore_wait(ready, 1)
         for i in range(parts):
             edge_up(i).start()
-
-    for d in range(1, parts):
-        grad_copy(1, d).start()
 
     def span(source, b):
         group = columns_of(source)

time: 31.5 us -> 32 us (1.016)
  Pallas kernels: 29.2 us -> 29.7 us
    pallas_call x1, Pallas kernels: 29.2 us -> 29.7 us  [shards(): pl.pallas_call(functools.partial(body, strips, parts, local), out_shape=j...]
where the time goes in v6:
time: 32 us; the launch traced here: 31.8 us
  Pallas kernels  29.7 us (93%)
  local copies, waits for them, and re-layouts  1.47 us (5%)
  between operations  0.66 us (2%)
    pallas_call x1, Pallas kernels, shards(): pl.pallas_call(functools.partial(body, strips, parts, local), out_shape=j...  29.7 us
    unnamed x1, local copies, waits for them, and re-layouts  1.47 us

profile of v6, /device:TPU:1, one launch (start us, length us, event | category | flops | bytes accessed | tf_op | source)
XLA Modules:
  0.0 31.8 jit_solution(659002834286582148)
XLA Ops:
  0.7 29.7 %shard_map.163 = f32[16,1024]{1,0:T(8,128)} custom-call(f32[128,1024]{1,0:T(8,128)} %mask_ref.1, s32[128,1024]{1,0:T(8,128)} %target_ref.1, f32[3,61,2,61]{3,2,1,0:T(2,128)} %bitcast.1, f32[3]{0:T(128)} %weight_ref.1, s32[1,2]{1,0:T(1,128)} %list_ref.1, s32[1]{0:T(128)S(6)} %copy.19.count_ref, bf16[160,384]{1,0:T(8,128)(2,1)} %constant.22.clone.rest_0_, ...), custom_call_target="tpu_custom_call" | custom-call | tf_op jit(solution)/shard_map/pallas_call | solution.py:513
  30.3 1.5 %copy.20 = f32[16,1024]{1,0:T(8,128)} copy(f32[16,1024]{1,0:T(8,128)} %shard_map.163) | data formatting | bytes 131072
